TPU v7x, 32 devices: a whole 2x2x4 slice. The times are simulated.
32 devices in a mesh: parts: 1, row: 8 (over z, y), col: 1, depth: 4 (over x, core).
Axes of the slice: x: 2, y: 2, z: 4, core: 2. Of those that a mesh axis runs over, the one named last changes fastest.
Arguments:
- activations: bfloat16 [4, 256, 8192], P(('parts', 'depth'), 'row', 'col'), may hold values from -6 to 6
- hidden_grads: bfloat16 [4, 256, 16384], P(('parts', 'depth'), 'col', 'row'), may hold values from -0.1875 to 0.1875
Outputs:
- weight_grad: bfloat16 [8192, 16384], P(('parts', 'col', 'depth'), 'row')
All inputs are finite; a program needn't handle non-finite values.
Results may differ from a plain program's by a relative error of at most 0.013.
Values may be sent and summed in bfloat16 or wider, within the bound.
A program may use at most 128 MiB of HBM per device.

v0:
```python
import jax
import jax.numpy as jnp
from jax import lax
from jax.sharding import PartitionSpec as P


def local(activations, hidden_grads):
    swapped = lax.all_to_all(activations, "depth", split_axis=2, concat_axis=0, tiled=True)
    acts = lax.all_gather(swapped, "row", axis=1, tiled=True)
    grads = lax.all_gather(hidden_grads, "depth", axis=0, tiled=True)
    grads = lax.all_gather(grads, "col", axis=1, tiled=True)
    total = lax.dot_general(
        acts, grads, (((0, 1), (0, 1)), ((), ())), preferred_element_type=jnp.float32
    )
    return total.astype(jnp.bfloat16)


def solution(mesh):
    in_specs = (P(("parts", "depth"), "row", "col"), P(("parts", "depth"), "col", "row"))
    out_specs = P(("parts", "col", "depth"), "row")
    return jax.shard_map(local, mesh=mesh, in_specs=in_specs, out_specs=out_specs, check_vma=False)
```

profile of v0, /device:TPU:0, one launch (start us, length us, event | category | flops | bytes accessed | tf_op | source)
XLA Modules:
  0.0 217.2 jit_solution(3695399159835913625)
XLA Ops:
  6.5 0.0 all-gather.6.cloned.1.call-start
  6.5 8.6 %copy.7 = bf16[1,32,8192]{1,0,2:T(2,128)(2,1)} copy(bf16[1,32,8192]{2,1,0:T(8,128)(2,1)} %param.2) | data formatting | bytes 1048576 | tf_op args[0]
  15.1 0.5 broadcast
  15.6 45.2 %reduce = bf16[8192,32]{1,0:T(8,128)(2,1)S(1)} reduce(bf16[8192,1,32]{2,1,0:T(2,128)(2,1)} %bitcast.11, bf16[]{:T(256)} %broadcast), dimensions={1}, to_apply=%bitcast.8.reduce_sub_computation | reduce | bytes 1048578
  60.8 2.2 reshape.2
  63.0 12.9 %all_to_all.18 = bf16[4,2,32768]{2,1,0:T(2,128)(2,1)S(1)} all-to-all(bf16[4,2,32768]{2,1,0:T(2,128)(2,1)S(1)} %reshape.2), channel_id=1, replica_groups=mesh['parts'=1,'row'=8,'col'=1,'depth'=4] {'depth'}, dimensions={0} | all-to-all | bytes 1048576 | tf_op jit(solution)/shard_map/all_to_all | solution.py:8
  75.9 3.3 %reshape.3 = bf16[8192,1,32]{2,1,0:T(2,128)(2,1)} reshape(bf16[4,2,32768]{2,1,0:T(2,128)(2,1)S(1)} %all_to_all.18) | data formatting | bytes 1048576
  79.1 8.0 %copy.8 = bf16[1,32,8192]{2,1,0:T(8,128)(2,1)S(1)} copy(bf16[1,32,8192]{1,0,2:T(2,128)(2,1)} %bitcast.12) | data formatting | bytes 1048576 | tf_op jit(solution)/shard_map/all_to_all | solution.py:8
  87.1 1.2 all_to_all.14
  88.3 0.0 all-gather.6.cloned.1.call-update
  88.3 0.2 all-gather.4.cloned.1.call-start
  88.5 0.5 all-gather.4.cloned.1.call-update
  89.0 73.1 %all-gather.6.cloned.1.call-done = bf16[4,1,256,2048]{3,0,1,2:T(4,128)(2,1)} async-done(((bf16[4,1,32,2048]{3,0,1,2:T(4,128)(2,1)}), bf16[4,1,256,2048]{3,0,1,2:T(4,128)(2,1)}) %all-gather.6.cloned.1.call-update) | async-done | bytes 4194320 | tf_op jit(solution)/shard_map/all_gather | solution.py:9
  162.2 7.6 %copy.10 = bf16[4,1,256,2048]{2,3,0,1:T(8,128)(2,1)} copy(bf16[4,1,256,2048]{3,0,1,2:T(4,128)(2,1)} %all-gather.6.cloned.1.call-done) | data formatting | bytes 8388608 | tf_op jit(solution)/shard_map/all_gather | solution.py:9
  169.7 26.8 %all-gather.4.cloned.1.call-done = bf16[4,256,2048]{2,1,0:T(8,128)(2,1)} async-done(((bf16[1,256,2048]{2,1,0:T(8,128)(2,1)}), bf16[4,256,2048]{2,1,0:T(8,128)(2,1)}) %all-gather.4.cloned.1.call-update) | async-done | bytes 4194320 | tf_op jit(solution)/shard_map/all_gather | solution.py:10
  196.5 13.9 %bitcast_convert_fusion = bf16[2048,2048]{1,0:T(8,128)(2,1)} fusion(bf16[4,256,2048]{2,1,0:T(8,128)(2,1)} %all-gather.4.cloned.1.call-done, bf16[4,1,256,2048]{2,3,0,1:T(8,128)(2,1)} %copy.10), kind=kOutput, calls=%fused_computation | convolution fusion | flops 8594128896 | bytes 16777216 | tf_op jit(solution)/shard_map/dot_general | solution.py:12
Async XLA Ops:
  6.5 155.6 %all-gather.6.cloned.1.call-start = ((), (), s32[]{:S(2)}) async-start(), calls=%async_computation.2 | async-start | bytes 4718592 | tf_op jit(solution)/shard_map/all_gather | solution.py:9
  88.3 108.2 %all-gather.4.cloned.1.call-start = ((), (), s32[]{:S(2)}) async-start(), calls=%async_computation.1 | async-start | bytes 5242880 | tf_op jit(solution)/shard_map/all_gather | solution.py:10
Sparse Core Ops, SparseCore 0:
  88.4 73.7 all-gather.5
  163.7 32.7 all-gather.3
where the time goes:
time: 218 us; the launch traced here: 217 us
  waiting for transfers between devices  100 us (46%)
  other arithmetic  45.2 us (21%)
  local copies, waits for them, and re-layouts  31.2 us (14%)
  matrix products  13.9 us (6%)
  between operations  13.4 us (6%)
  blocking collectives  12.9 us (6%)
    all_gather x1, waiting for transfers between devices, local(): acts = lax.all_gather(swapped, 'row', axis=1, tiled=True)  73.1 us
    unnamed x1, other arithmetic  45.2 us
    all_gather x1, waiting for transfers between devices, local(): grads = lax.all_gather(hidden_grads, 'depth', axis=0, tiled=True)  26.8 us
    unnamed x4, local copies, waits for them, and re-layouts  14.5 us
    dot_general x1, matrix products, local(): lax.dot_general(acts, grads, (((0, 1), (0, 1)), ((), ())), preferred_elem...  13.9 us
    all_to_all x1, blocking collectives, local(): lax.all_to_all(activations, 'depth', split_axis=2, concat_axis=0, tiled=T...  12.9 us
    all_to_all x2, local copies, waits for them, and re-layouts, local(): lax.all_to_all(activations, 'depth', split_axis=2, concat_axis=0, tiled=T...  9.14 us
    all_gather x1, local copies, waits for them, and re-layouts, local(): acts = lax.all_gather(swapped, 'row', axis=1, tiled=True)  7.56 us
  transfers between devices with their start and end apart: 2, of which 2 were waited for; matrix products, arithmetic and copies ran while one was open for 3% of the time, Pallas kernels for 0%

commit v1 on v0

--- a/solution.py
+++ b/solution.py
@@ -6,7 +6,12 @@
 
 def local(activations, hidden_grads):
     swapped = lax.all_to_all(activations, "depth", split_axis=2, concat_axis=0, tiled=True)
-    acts = lax.all_gather(swapped, "row", axis=1, tiled=True)
+    ring = [swapped]
+    for hop in range(7):
+        ring.append(lax.ppermute(ring[-1], "row", [(dev, (dev + 1) % 8) for dev in range(8)]))
+    acts = jnp.roll(
+        jnp.concatenate(ring[::-1], axis=1), (lax.axis_index("row") + 1) * ring[0].shape[1], axis=1
+    )
     grads = lax.all_gather(hidden_grads, "depth", axis=0, tiled=True)
     grads = lax.all_gather(grads, "col", axis=1, tiled=True)
     total = lax.dot_general(

time: 218 us -> 242 us (1.11); the launches traced: 217 us -> 238 us
  local copies, waits for them, and re-layouts: 31.2 us -> 67.7 us
  waiting for transfers between devices: 100 us -> 83.1 us
    ppermute x0 -> x7, waiting for transfers between devices: none -> 82.3 us  [local(): lax.ppermute(ring[-1], 'row', [(dev, (dev + 1) % 8) for dev in range(8)])]
    all_gather x1 -> x0, waiting for transfers between devices: 73.1 us -> none  [local(): acts = lax.all_gather(swapped, 'row', axis=1, tiled=True)]
    concatenate x0 -> x1, local copies, waits for them, and re-layouts: none -> 32.6 us  [local(): jnp.roll(jnp.concatenate(ring[::-1], axis=1), (lax.axis_index('row') + 1)...]
    all_gather x1, waiting for transfers between devices: 26.8 us -> 0.02 us  [local(): grads = lax.all_gather(hidden_grads, 'depth', axis=0, tiled=True)]
    ppermute x0 -> x7, local copies, waits for them, and re-layouts: none -> 14.9 us  [local(): lax.ppermute(ring[-1], 'row', [(dev, (dev + 1) % 8) for dev in range(8)])]
    all_to_all x2 -> x1, local copies, waits for them, and re-layouts: 9.14 us -> 0.8 us  [local(): lax.all_to_all(activations, 'depth', split_axis=2, concat_axis=0, tiled=T...]
    all_gather x1 -> x0, local copies, waits for them, and re-layouts: 7.56 us -> none  [local(): acts = lax.all_gather(swapped, 'row', axis=1, tiled=True)]
    unnamed x4 -> x15, local copies, waits for them, and re-layouts: 14.5 us -> 19.4 us
  transfers between devices with their start and end apart: 2 -> 8, of which waited for: 2 -> 6; matrix products, arithmetic and copies ran while one was open for 3% -> 46% of each run, Pallas kernels for 0% -> 0%
where the time goes in v1:
time: 242 us; the launch traced here: 238 us
  waiting for transfers between devices  83.1 us (34%)
  local copies, waits for them, and re-layouts  67.7 us (28%)
  other arithmetic  45.3 us (19%)
  matrix products  14.3 us (6%)
  between operations  13.4 us (6%)
  blocking collectives  12.9 us (5%)
    ppermute x7, waiting for transfers between devices, local(): lax.ppermute(ring[-1], 'row', [(dev, (dev + 1) % 8) for dev in range(8)])  82.3 us
    unnamed x1, other arithmetic  45.3 us
    concatenate x1, local copies, waits for them, and re-layouts, local(): jnp.roll(jnp.concatenate(ring[::-1], axis=1), (lax.axis_index('row') + 1)...  32.6 us
    unnamed x15, local copies, waits for them, and re-layouts  19.4 us
    ppermute x7, local copies, waits for them, and re-layouts, local(): lax.ppermute(ring[-1], 'row', [(dev, (dev + 1) % 8) for dev in range(8)])  14.9 us
    dot_general x1, matrix products, local(): lax.dot_general(acts, grads, (((0, 1), (0, 1)), ((), ())), preferred_elem...  14.3 us
    all_to_all x1, blocking collectives, local(): lax.all_to_all(activations, 'depth', split_axis=2, concat_axis=0, tiled=T...  12.9 us
  transfers between devices with their start and end apart: 8, of which 6 were waited for; matrix products, arithmetic and copies ran while one was open for 46% of the time, Pallas kernels for 0%

profile of v1, /device:TPU:0, one launch (start us, length us, event | category | flops | bytes accessed | tf_op | source)
XLA Modules:
  0.0 238.2 jit_solution(13885267524482324199)
XLA Ops:
  6.5 0.0 all-gather.2.cloned.1.call-start
  6.5 0.7 all-gather.2.cloned.1.call-update
  7.3 8.6 %copy.20 = bf16[1,32,8192]{1,0,2:T(2,128)(2,1)} copy(bf16[1,32,8192]{2,1,0:T(8,128)(2,1)} %param.2) | data formatting | bytes 1048576 | tf_op args[0]
  15.8 0.5 broadcast.1
  16.4 45.3 %reduce = bf16[8192,32]{1,0:T(8,128)(2,1)S(1)} reduce(bf16[8192,1,32]{2,1,0:T(2,128)(2,1)} %bitcast.13, bf16[]{:T(256)} %broadcast.1), dimensions={1}, to_apply=%bitcast.7.reduce_sub_computation | reduce | bytes 1048578
  61.6 2.2 reshape.2
  63.8 12.9 %all_to_all.18 = bf16[4,2,32768]{2,1,0:T(2,128)(2,1)S(1)} all-to-all(bf16[4,2,32768]{2,1,0:T(2,128)(2,1)S(1)} %reshape.2), channel_id=1, replica_groups=mesh['parts'=1,'row'=8,'col'=1,'depth'=4] {'depth'}, dimensions={0} | all-to-all | bytes 1048576 | tf_op jit(solution)/shard_map/all_to_all | solution.py:8
  76.7 3.3 %reshape.3 = bf16[8192,1,32]{2,1,0:T(2,128)(2,1)} reshape(bf16[4,2,32768]{2,1,0:T(2,128)(2,1)S(1)} %all_to_all.18) | data formatting | bytes 1048576
  79.9 2.5 %copy.38 = bf16[1,32,8192]{1,2,0:T(8,128)(2,1)S(1)} copy(bf16[1,32,8192]{1,0,2:T(2,128)(2,1)} %bitcast.14) | data formatting | bytes 1048576
  82.4 0.8 copy.23
  83.2 1.6 collective-permute-start
  84.8 14.6 %collective-permute-done = bf16[4,32,2048]{2,1,0:T(8,128)(2,1)S(1)} collective-permute-done((bf16[4,32,2048]{2,1,0:T(8,128)(2,1)S(1)}, bf16[4,32,2048]{2,1,0:T(8,128)(2,1)S(1)}, u32[]{:S(2)}, u32[]{:S(2)}) %collective-permute-start) | collective-permute-done | bytes 524320 | tf_op jit(solution)/shard_map/ppermute | solution.py:11
  99.4 0.0 collective-permute-start.1
  99.4 15.2 %collective-permute-done.1 = bf16[4,32,2048]{2,1,0:T(8,128)(2,1)S(1)} collective-permute-done((bf16[4,32,2048]{2,1,0:T(8,128)(2,1)S(1)}, bf16[4,32,2048]{2,1,0:T(8,128)(2,1)S(1)}, u32[]{:S(2)}, u32[]{:S(2)}) %collective-permute-start.1) | collective-permute-done | bytes 524320 | tf_op jit(solution)/shard_map/ppermute | solution.py:11
  114.6 0.0 collective-permute-start.2
  114.6 14.3 %collective-permute-done.2 = bf16[4,32,2048]{2,1,0:T(8,128)(2,1)S(1)} collective-permute-done((bf16[4,32,2048]{2,1,0:T(8,128)(2,1)S(1)}, bf16[4,32,2048]{2,1,0:T(8,128)(2,1)S(1)}, u32[]{:S(2)}, u32[]{:S(2)}) %collective-permute-start.2) | collective-permute-done | bytes 524320 | tf_op jit(solution)/shard_map/ppermute | solution.py:11
  128.9 0.0 copy-start
  128.9 0.8 copy-done
  129.7 0.0 collective-permute-start.3
  129.7 13.4 %collective-permute-done.3 = bf16[4,32,2048]{2,1,0:T(8,128)(2,1)S(1)} collective-permute-done((bf16[4,32,2048]{2,1,0:T(8,128)(2,1)S(1)}, bf16[4,32,2048]{2,1,0:T(8,128)(2,1)S(1)}, u32[]{:S(2)}, u32[]{:S(2)}) %collective-permute-start.3) | collective-permute-done | bytes 524320 | tf_op jit(solution)/shard_map/ppermute | solution.py:11
  143.0 0.0 copy-start.1
  143.0 0.8 copy-done.1
  143.9 0.0 collective-permute-start.4
  143.9 12.4 %collective-permute-done.4 = bf16[4,32,2048]{2,1,0:T(8,128)(2,1)S(1)} collective-permute-done((bf16[4,32,2048]{2,1,0:T(8,128)(2,1)S(1)}, bf16[4,32,2048]{2,1,0:T(8,128)(2,1)S(1)}, u32[]{:S(2)}, u32[]{:S(2)}) %collective-permute-start.4) | collective-permute-done | bytes 524320 | tf_op jit(solution)/shard_map/ppermute | solution.py:11
  156.3 0.0 copy-start.3
  156.3 0.8 copy-done.3
  157.1 0.0 collective-permute-start.5
  157.1 12.5 %collective-permute-done.5 = bf16[4,32,2048]{2,1,0:T(8,128)(2,1)} collective-permute-done((bf16[4,32,2048]{2,1,0:T(8,128)(2,1)S(1)}, bf16[4,32,2048]{2,1,0:T(8,128)(2,1)}, u32[]{:S(2)}, u32[]{:S(2)}) %collective-permute-start.5) | collective-permute-done | bytes 524320 | tf_op jit(solution)/shard_map/ppermute | solution.py:11
  169.6 0.0 collective-permute-start.6
  169.6 1.8 copy.30
  171.3 0.0 copy-start.2
  171.3 1.7 copy.29
  173.0 0.0 copy-start.4
  173.0 2.7 %copy.28 = bf16[4,32,2048]{1,2,0:T(8,128)(2,1)} copy(bf16[4,32,2048]{2,1,0:T(8,128)(2,1)} %copy-done) | data formatting | bytes 1048576 | tf_op jit(solution)/shard_map/ppermute | solution.py:11
  175.7 0.0 copy-done.2
  175.7 1.8 copy.27
  177.5 0.0 copy-done.4
  177.5 1.7 copy.26
  179.2 2.6 %copy.25 = bf16[4,32,2048]{1,2,0:T(8,128)(2,1)} copy(bf16[4,32,2048]{2,1,0:T(8,128)(2,1)} %collective-permute-done.5) | data formatting | bytes 1048576 | tf_op jit(solution)/shard_map/ppermute | solution.py:11
  181.9 0.0 collective-permute-done.6
  181.9 2.6 %copy.24 = bf16[4,32,2048]{1,2,0:T(8,128)(2,1)} copy(bf16[4,32,2048]{2,1,0:T(8,128)(2,1)} %collective-permute-done.6) | data formatting | bytes 1048576 | tf_op jit(solution)/shard_map/ppermute | solution.py:11
  184.5 32.6 %concatenate.6 = bf16[4,512,2048]{1,2,0:T(8,128)(2,1)} concatenate(bf16[4,32,2048]{1,2,0:T(8,128)(2,1)} %copy.24, bf16[4,32,2048]{1,2,0:T(8,128)(2,1)} %copy.25, bf16[4,32,2048]{1,2,0:T(8,128)(2,1)} %copy.26, bf16[4,32,2048]{1,2,0:T(8,128)(2,1)} %copy.27, bf16[4,32,2048]{1,2,0:T(8,128)(2,1)} %copy.28, bf16[4,32,2048]{1,2,0:T(8,128)(2,1)} %copy.29, bf16[4,32,2048]{1,2,0:T(8,128)(2,1)} %copy.30, ...), dimensions={1} | concatenate | bytes 16777216 | tf_op jit(solution)/shard_map/jit(_roll_dynamic)/concatenate | solution.py:12
  217.1 0.0 all-gather.2.cloned.1.call-done
  217.1 14.3 %bitcast_convert_fusion = bf16[2048,2048]{1,0:T(8,128)(2,1)} fusion(bf16[4,256,2048]{2,1,0:T(8,128)(2,1)} %all-gather.2.cloned.1.call-done, bf16[4,512,2048]{1,2,0:T(8,128)(2,1)} %concatenate.6, s32[]{:T(128)S(6)} %select_n.14), kind=kOutput, calls=%fused_computation | convolution fusion | flops 8594128896 | bytes 16777220 | tf_op jit(solution)/shard_map/dot_general | solution.py:17
Async XLA Ops:
  6.5 210.6 %all-gather.2.cloned.1.call-start = ((), (), s32[]{:S(2)}) async-start(), calls=%async_computation.1 | async-start | bytes 5242880 | tf_op jit(solution)/shard_map/all_gather | solution.py:15
  83.2 16.2 %collective-permute-start = (bf16[4,32,2048]{2,1,0:T(8,128)(2,1)S(1)}, bf16[4,32,2048]{2,1,0:T(8,128)(2,1)S(1)}, u32[]{:S(2)}, u32[]{:S(2)}) collective-permute-start(bf16[4,32,2048]{2,1,0:T(8,128)(2,1)S(1)} %copy.23), channel_id=1, source_target_pairs={{0,4},{4,8},{8,12},{12,16},{16,20},{20,24},{24,28},{28,0},{1,5},{5... | collective-permute-start | bytes 1572872 | tf_op jit(solution)/shard_map/ppermute | solution.py:11
  99.4 15.2 %collective-permute-start.1 = (bf16[4,32,2048]{2,1,0:T(8,128)(2,1)S(1)}, bf16[4,32,2048]{2,1,0:T(8,128)(2,1)S(1)}, u32[]{:S(2)}, u32[]{:S(2)}) collective-permute-start(bf16[4,32,2048]{2,1,0:T(8,128)(2,1)S(1)} %collective-permute-done), channel_id=1, source_target_pairs={{0,4},{4,8},{8,12},{12,16},{16,20},{20,24},{24,28},{28,0},{1,5},{5... | collective-permute-start | bytes 1572872 | tf_op jit(solution)/shard_map/ppermute | solution.py:11
  114.6 14.3 %collective-permute-start.2 = (bf16[4,32,2048]{2,1,0:T(8,128)(2,1)S(1)}, bf16[4,32,2048]{2,1,0:T(8,128)(2,1)S(1)}, u32[]{:S(2)}, u32[]{:S(2)}) collective-permute-start(bf16[4,32,2048]{2,1,0:T(8,128)(2,1)S(1)} %collective-permute-done.1), channel_id=1, source_target_pairs={{0,4},{4,8},{8,12},{12,16},{16,20},{20,24},{24,28},{28,0},{1,5},{5... | collective-permute-start | bytes 1572872 | tf_op jit(solution)/shard_map/ppermute | solution.py:11
  128.9 0.8 copy-start
  129.7 13.4 %collective-permute-start.3 = (bf16[4,32,2048]{2,1,0:T(8,128)(2,1)S(1)}, bf16[4,32,2048]{2,1,0:T(8,128)(2,1)S(1)}, u32[]{:S(2)}, u32[]{:S(2)}) collective-permute-start(bf16[4,32,2048]{2,1,0:T(8,128)(2,1)S(1)} %collective-permute-done.2), channel_id=1, source_target_pairs={{0,4},{4,8},{8,12},{12,16},{16,20},{20,24},{24,28},{28,0},{1,5},{5... | collective-permute-start | bytes 1572872 | tf_op jit(solution)/shard_map/ppermute | solution.py:11
  143.0 0.8 copy-start.1
  143.9 12.4 %collective-permute-start.4 = (bf16[4,32,2048]{2,1,0:T(8,128)(2,1)S(1)}, bf16[4,32,2048]{2,1,0:T(8,128)(2,1)S(1)}, u32[]{:S(2)}, u32[]{:S(2)}) collective-permute-start(bf16[4,32,2048]{2,1,0:T(8,128)(2,1)S(1)} %collective-permute-done.3), channel_id=1, source_target_pairs={{0,4},{4,8},{8,12},{12,16},{16,20},{20,24},{24,28},{28,0},{1,5},{5... | collective-permute-start | bytes 1572872 | tf_op jit(solution)/shard_map/ppermute | solution.py:11
  156.3 0.8 copy-start.3
  157.1 12.5 %collective-permute-start.5 = (bf16[4,32,2048]{2,1,0:T(8,128)(2,1)S(1)}, bf16[4,32,2048]{2,1,0:T(8,128)(2,1)}, u32[]{:S(2)}, u32[]{:S(2)}) collective-permute-start(bf16[4,32,2048]{2,1,0:T(8,128)(2,1)S(1)} %collective-permute-done.4), channel_id=1, source_target_pairs={{0,4},{4,8},{8,12},{12,16},{16,20},{20,24},{24,28},{28,0},{1,5},{5... | collective-permute-start | bytes 1572872 | tf_op jit(solution)/shard_map/ppermute | solution.py:11
  169.6 12.3 %collective-permute-start.6 = (bf16[4,32,2048]{2,1,0:T(8,128)(2,1)}, bf16[4,32,2048]{2,1,0:T(8,128)(2,1)}, u32[]{:S(2)}, u32[]{:S(2)}) collective-permute-start(bf16[4,32,2048]{2,1,0:T(8,128)(2,1)} %collective-permute-done.5), channel_id=1, source_target_pairs={{0,4},{4,8},{8,12},{12,16},{16,20},{20,24},{24,28},{28,0},{1,5},{5... | collective-permute-start | bytes 1572872 | tf_op jit(solution)/shard_map/ppermute | solution.py:11
  171.3 4.4 %copy-start.2 = (bf16[4,32,2048]{2,1,0:T(8,128)(2,1)S(1)}, bf16[4,32,2048]{2,1,0:T(8,128)(2,1)}, u32[]{:S(2)}) copy-start(bf16[4,32,2048]{2,1,0:T(8,128)(2,1)} %copy-done.1) | copy-start | bytes 1572868
  173.0 4.4 %copy-start.4 = (bf16[4,32,2048]{2,1,0:T(8,128)(2,1)S(1)}, bf16[4,32,2048]{2,1,0:T(8,128)(2,1)}, u32[]{:S(2)}) copy-start(bf16[4,32,2048]{2,1,0:T(8,128)(2,1)} %copy-done.3) | copy-start | bytes 1572868
Sparse Core Ops, SparseCore 0:
  8.9 37.1 all-gather.1
